TPU v7x, 32 devices: a whole 2x2x4 slice. The times are simulated.
32 devices in a mesh: tm: 4 (over y, x), space: 8 (over z, core).
Axes of the slice: x: 2, y: 2, z: 4, core: 2. Of those that a mesh axis runs over, the one named last changes fastest.
Arguments:
- material_ids: int32 [128, 2048], P('space'), may hold values from 0 to 7
- conductivity_table: float32 [8], replicated, may hold values from 0.1 to 10
- c_points: float32 [4, 128, 2048], P('tm', 'space'), may hold values from -6 to 6
Outputs:
- f_points: float32 [4, 128, 2048], P('tm', 'space')
- next_c: float32 [4, 128, 2048], P('tm', 'space')
All inputs are finite; a program needn't handle non-finite values.
Results may differ from a plain program's by a relative error of at most 0.00022.
Values sent between devices are 32-bit elements; how exact they have to be, the bound alone decides.
A program may use at most 64 MiB of HBM per device.

v0:
```python
import functools

import jax
import jax.numpy as jnp
from jax import lax
from jax.experimental import pallas as pl
from jax.experimental.pallas import tpu as pltpu
from jax.sharding import PartitionSpec as P

MESH = pl.DeviceIdType.MESH
MATS = 8
COARSE_SWEEPS = 16
DIFFUSION = 1024.0
HALO = 12
H1 = HALO // 2
PAD = 2


def rows_loop(lo, hi, size, body):
    count = hi - lo
    full = count // size
    if full == 1:
        body(lo, size)
    elif full > 1:

        def step(i, carry):
            body(lo + i * size, size)
            return carry

        lax.fori_loop(0, full, step, 0)
    if count % size:
        body(lo + full * size, count % size)


def iota(shape, dim):
    return lax.broadcasted_iota(jnp.int32, shape, dim)


def roll(x, by, axis):
    return pltpu.roll(x, by, axis)


def from_west(x, d):
    r = roll(x, d, 2)
    return jnp.where(iota(x.shape, 2) < d, roll(r, 1, 1), r)


def from_east(x, d):
    r = roll(x, 128 - d, 2)
    return jnp.where(iota(x.shape, 2) >= 128 - d, roll(r, 7, 1), r)


def first_col(shape, d):
    return (iota(shape, 1) == 0) & (iota(shape, 2) < d)


def last_col(shape, d):
    return (iota(shape, 1) == 7) & (iota(shape, 2) >= 128 - d)


def partner(x, d):
    return jnp.where((iota(x.shape, 2) & d) == 0, roll(x, 128 - d, 2), roll(x, d, 2))


def pair_rows(x):
    x = x.reshape((x.shape[0] // 2, 2) + x.shape[1:])
    return x[:, 0], x[:, 1]


def restrict(x, d):
    a, b = pair_rows(x)
    t = a + b
    return 0.25 * (t + partner(t, d))


def split3(x):
    hi = x.astype(jnp.bfloat16)
    rest = x - hi.astype(jnp.float32)
    mid = rest.astype(jnp.bfloat16)
    lo = (rest - mid.astype(jnp.float32)).astype(jnp.bfloat16)
    return hi, mid, lo


def dot(a, b):
    return jnp.dot(a, b, preferred_element_type=jnp.float32)


class Level:
    def __init__(self, refs, d, scale, size):
        self.cond, self.fv, self.w, self.e, self.diag, self.om, self.g, self.b, self.c = refs
        self.d, self.scale, self.size = d, scale, size

    def setup(self, lo, hi, first_row, last_row, base):
        d, half = self.d, self.scale * 0.5

        def body(r, c):
            cond = self.cond
            here = cond[pl.ds(r, c)]
            shape = here.shape
            n = half * (here + cond[pl.ds(r - 1, c)])
            s = half * (here + cond[pl.ds(r + 1, c)])
            out_w, out_e = first_col(shape, d), last_col(shape, d)
            w = half * (here + jnp.where(out_w, 0.0, from_west(here, d)))
            e = half * (here + jnp.where(out_e, 0.0, from_east(here, d)))
            diag = 1.0 + ((n + s) + (w + e))
            row = iota(shape, 0) + (r + base)
            self.fv[pl.ds(r, c)] = jnp.where((row > first_row) & (row <= last_row), n, 0.0)
            self.w[pl.ds(r, c)] = jnp.where(out_w, 0.0, w)
            self.e[pl.ds(r, c)] = jnp.where(out_e, 0.0, e)
            self.diag[pl.ds(r, c)] = diag
            self.om[pl.ds(r, c)] = 0.8 / diag

        rows_loop(lo, hi, self.size, body)

    def beside(self, v, r, c):
        here = v[pl.ds(r, c)]
        nb = (
            self.fv[pl.ds(r, c)] * v[pl.ds(r - 1, c)]
            + self.fv[pl.ds(r + 1, c)] * v[pl.ds(r + 1, c)]
        ) + (
            self.w[pl.ds(r, c)] * from_west(here, self.d)
            + self.e[pl.ds(r, c)] * from_east(here, self.d)
        )
        return here, nb

    def start(self, lo, hi, dst):
        def body(r, c):
            dst[pl.ds(r, c)] = self.om[pl.ds(r, c)] * self.g[pl.ds(r, c)]

        rows_loop(lo, hi, self.size, body)

    def sweep(self, lo, hi, src, dst):
        def body(r, c):
            here, nb = self.beside(src, r, c)
            dst[pl.ds(r, c)] = 0.2 * here + self.om[pl.ds(r, c)] * (self.g[pl.ds(r, c)] + nb)

        rows_loop(lo, hi, self.size, body)

    def residue(self, v, r, c):
        here, nb = self.beside(v, r, c)
        return self.g[pl.ds(r, c)] - (self.diag[pl.ds(r, c)] * here - nb)


def kernel(
    n, intervals, ny,
    ids_ref, table_ref, c_ref, f_ref, out_ref,
    turn, start_w, first_w, b0, c0, cond0, fv0, w0, e0, diag0, om0,
    cond1, fv1, w1, e1, diag1, om1, g1, b1, c1,
    cond2, fv2, w2, e2, diag2, om2, g2, b2, c2,
    cond3, fv3, w3, e3, diag3, om3, g3, b3, c3,
    cond4, fv4, w4, e4, diag4, om4, g4, b4, c4,
    gather_cond, gather_1, gather_2, end_nat,
    halo_send, halo_recv, gat_send, gat_recv, end_send, end_recv,
):
    me = lax.axis_index("space")
    mine_t = lax.axis_index("tm")
    R = c_ref.shape[1]
    top, bottom = HALO, HALO + R
    window = R + 2 * HALO

    barrier = pltpu.get_barrier_semaphore()
    for j in range(1, n):
        pl.semaphore_signal(barrier, 1, device_id={"space": lax.rem(me + j, n)}, device_id_type=MESH)

    for j in (1, intervals - 1):
        next_t = lax.rem(mine_t + j, intervals)
        pl.semaphore_signal(barrier, 1, device_id={"tm": next_t}, device_id_type=MESH)

    def halo_copies(ref, which):
        up = pltpu.make_async_remote_copy(
            src_ref=ref.at[pl.ds(top, HALO)],
            dst_ref=ref.at[pl.ds(bottom, HALO)],
            send_sem=halo_send.at[2 * which],
            recv_sem=halo_recv.at[2 * which],
            device_id={"space": lax.rem(me + n - 1, n)},
            device_id_type=MESH,
        )
        down = pltpu.make_async_remote_copy(
            src_ref=ref.at[pl.ds(bottom - HALO, HALO)],
            dst_ref=ref.at[pl.ds(0, HALO)],
            send_sem=halo_send.at[2 * which + 1],
            recv_sem=halo_recv.at[2 * which + 1],
            device_id={"space": lax.rem(me + 1, n)},
            device_id_type=MESH,
        )
        return up, down

    def halo_start(ref, which):
        up, down = halo_copies(ref, which)

        @pl.when(me > 0)
        def _():
            up.start()

        @pl.when(me < n - 1)
        def _():
            down.start()

    def halo_arrive(ref, which):
        up, down = halo_copies(ref, which)
        zero = jnp.zeros((HALO,) + ref.shape[1:], jnp.float32)

        @pl.when(me > 0)
        def _():
            down.wait_recv()

        @pl.when(me == 0)
        def _():
            ref[pl.ds(0, HALO)] = zero

        @pl.when(me < n - 1)
        def _():
            up.wait_recv()

        @pl.when(me == n - 1)
        def _():
            ref[pl.ds(bottom, HALO)] = zero

    def halo_sent(ref, which):
        up, down = halo_copies(ref, which)

        @pl.when(me > 0)
        def _():
            up.wait_send()

        @pl.when(me < n - 1)
        def _():
            down.wait_send()

    def gather_copy(ref, which, j, slot):
        return pltpu.make_async_remote_copy(
            src_ref=ref.at[slot],
            dst_ref=ref.at[slot],
            send_sem=gat_send.at[which * n + j],
            recv_sem=gat_recv.at[which * n + j],
            device_id={"space": lax.rem(me + j, n)},
            device_id_type=MESH,
        )

    def gather_start(ref, which):
        for j in range(1, n):
            gather_copy(ref, which, j, me).start()

    def gather_arrive(ref, which):
        for j in range(1, n):
            gather_copy(ref, which, j, lax.rem(me + n - j, n)).wait_recv()

    def gather_sent(ref, which):
        for j in range(1, n):
            gather_copy(ref, which, j, me).wait_send()

    row_i, col_i = iota((256, 256), 0), iota((256, 256), 1)
    into = jnp.where(col_i == (row_i & 1) * 128 + (row_i >> 1), 1.0, 0.0).astype(jnp.bfloat16)

    def put_turned(y):
        for k in range(2):
            turn[pl.ds(k * 8 * R, 8 * R), :] = y[:, k * 128 : (k + 1) * 128]

    def chunks(x):
        return jnp.concatenate([x[:, s * 256 : (s + 1) * 256] for s in range(8)], axis=0)

    put_turned(dot(chunks(ids_ref[...].astype(jnp.float32)).astype(jnp.bfloat16), into))
    for r in range(R):
        for k in range(2):
            kind = turn[pl.ds(k * 8 * R + r, 8, stride=R), :]
            value = jnp.zeros((8, 128), jnp.float32)
            for m in range(MATS):
                value = jnp.where(kind == float(m), table_ref[m], value)
            cond0[top + r, k] = value

    put_turned(sum(dot(part, into) for part in split3(chunks(c_ref[0]))))
    for r in range(R):
        for k in range(2):
            start_w[top + r, k] = turn[pl.ds(k * 8 * R + r, 8, stride=R), :]

    def natural(src, row0, store):
        for r in range(R):
            for k in range(2):
                turn[pl.ds(k * 8 * R + r, 8, stride=R), :] = src[row0 + r, k]
        back = jnp.where(row_i == (col_i & 1) * 128 + (col_i >> 1), 1.0, 0.0).astype(jnp.bfloat16)
        x = jnp.concatenate(
            [turn[pl.ds(0, 8 * R), :], turn[pl.ds(8 * R, 8 * R), :]], axis=1
        )
        y = sum(dot(part, back) for part in split3(x))
        for s in range(8):
            store(s, y[s * R : (s + 1) * R])

    pl.semaphore_wait(barrier, n + 1)

    halo_start(cond0, 0)
    halo_start(start_w, 1)

    scale = DIFFUSION
    L1 = Level((cond1, fv1, w1, e1, diag1, om1, g1, b1, c1), 1, scale / 4, 7)
    L2 = Level((cond2, fv2, w2, e2, diag2, om2, g2, b2, c2), 2, scale / 16, 8)
    L3 = Level((cond3, fv3, w3, e3, diag3, om3, g3, b3, c3), 4, scale / 64, 8)
    L4 = Level((cond4, fv4, w4, e4, diag4, om4, g4, b4, c4), 8, scale / 256, 8)
    ny2, ny3, ny4 = ny // 4, ny // 8, ny // 16

    def coarsen_cond(lo, hi):
        def body(j, c):
            x = cond0[pl.ds(2 * j, 2 * c)]
            a, b = pair_rows(x)
            t = a + b
            cond1[pl.ds(j, c)] = 0.25 * (t[:, 0] + t[:, 1])

        rows_loop(lo, hi, 4, body)

    coarsen_cond(H1, H1 + R // 2)
    gather_cond[me] = pack4(restrict(cond1[pl.ds(H1, R // 2)], 1))
    gather_start(gather_cond, 0)

    zero_pad = jnp.zeros((PAD, 8, 128), jnp.float32)
    for level, rows in ((L2, ny2), (L3, ny3), (L4, ny4)):
        for ref in (level.cond, level.b, level.c, level.fv):
            ref[pl.ds(0, PAD)] = zero_pad
            ref[pl.ds(PAD + rows, PAD)] = zero_pad

    gather_arrive(gather_cond, 0)
    unpack4(gather_cond, cond2)
    cond3[pl.ds(PAD, ny3)] = restrict(cond2[pl.ds(PAD, ny2)], 2)
    cond4[pl.ds(PAD, ny4)] = restrict(cond3[pl.ds(PAD, ny3)], 4)
    for level, rows in ((L2, ny2), (L3, ny3), (L4, ny4)):
        level.setup(PAD, PAD + rows, 0, rows - 1, -PAD)

    halo_arrive(cond0, 0)
    coarsen_cond(0, H1)
    coarsen_cond(H1 + R // 2, R // 2 + 2 * H1)
    base0 = me * R - HALO
    half0 = scale * 0.5

    def setup0(r, c):
        here0, here1 = cond0[pl.ds(r, c), 0], cond0[pl.ds(r, c), 1]
        shape = here0.shape
        out_w, out_e = first_col(shape, 1), last_col(shape, 1)
        mid = half0 * (here0 + here1)
        west = half0 * (here0 + jnp.where(out_w, 0.0, from_west(here1, 1)))
        east = half0 * (here1 + jnp.where(out_e, 0.0, from_east(here0, 1)))
        row = iota(shape, 0) + (r + base0)
        inside = (row > 0) & (row <= ny - 1)
        for k, here, we in ((0, here0, west + mid), (1, here1, mid + east)):
            north = half0 * (here + cond0[pl.ds(r - 1, c), k])
            south = half0 * (here + cond0[pl.ds(r + 1, c), k])
            diag = 1.0 + ((north + south) + we)
            fv0[pl.ds(r, c), k] = jnp.where(inside, north, 0.0)
            diag0[pl.ds(r, c), k] = diag
            om0[pl.ds(r, c), k] = 0.8 / diag
        w0[pl.ds(r, c), 0] = jnp.where(out_w, 0.0, west)
        w0[pl.ds(r, c), 1] = mid
        e0[pl.ds(r, c)] = jnp.where(out_e, 0.0, east)

    rows_loop(1, window - 1, 4, setup0)
    L1.setup(1, R // 2 + 2 * H1 - 1, 0, ny // 2 - 1, me * (R // 2) - H1)

    def beside0(v, r, c):
        v0, v1 = v[pl.ds(r, c), 0], v[pl.ds(r, c), 1]
        up, down = pl.ds(r - 1, c), pl.ds(r + 1, c)
        at = pl.ds(r, c)
        mid = w0[at, 1]
        nb0 = (fv0[at, 0] * v[up, 0] + fv0[down, 0] * v[down, 0]) + (
            w0[at, 0] * from_west(v1, 1) + mid * v1
        )
        nb1 = (fv0[at, 1] * v[up, 1] + fv0[down, 1] * v[down, 1]) + (
            mid * v0 + e0[at] * from_east(v0, 1)
        )
        return (v0, v1), (nb0, nb1)

    def sweep0(lo, hi, src, g, dst):
        def body(r, c):
            here, nb = beside0(src, r, c)
            at = pl.ds(r, c)
            for k in range(2):
                dst[at, k] = 0.2 * here[k] + om0[at, k] * (g[at, k] + nb[k])

        rows_loop(lo, hi, 6, body)

    def vcycle(g0, gathered, which, dst):
        sweep0(top - 10, bottom + 10, g0, g0, b0)
        sweep0(top - 9, bottom + 9, b0, g0, c0)

        def to_level_1(j, c):
            r, rows = 2 * j, 2 * c
            here, nb = beside0(c0, r, rows)
            at = pl.ds(r, rows)
            r0 = g0[at, 0] - (diag0[at, 0] * here[0] - nb[0])
            r1 = g0[at, 1] - (diag0[at, 1] * here[1] - nb[1])
            a, b = pair_rows(r0 + r1)
            g1[pl.ds(j, c)] = 0.25 * (a + b)

        own1, end1 = H1, H1 + R // 2
        rows_loop(own1 - 4, end1 + 4, 4, to_level_1)
        L1.start(own1 - 4, end1 + 4, b1)
        L1.sweep(own1 - 3, end1 + 3, b1, c1)
        gathered[me] = pack4(restrict(L1.residue(c1, own1, R // 2), 1))
        gather_start(gathered, which)
        gather_arrive(gathered, which)
        unpack4(gathered, g2)

        def down(level, rows, coarse):
            level.start(PAD, PAD + rows, level.b)
            level.sweep(PAD, PAD + rows, level.b, level.c)

            def body(j, c):
                coarse.g[pl.ds(PAD + j, c)] = restrict(
                    level.residue(level.c, PAD + 2 * j, 2 * c), level.d
                )

            rows_loop(0, rows // 2, 4, body)

        def up(level, rows, e_ref):
            def body(j, c):
                at = pl.ds(PAD + 2 * j, 2 * c)
                e = e_ref[pl.ds(PAD + j, c)]
                twice = jnp.stack([e, e], axis=1).reshape((2 * c, 8, 128))
                level.c[at] = level.c[at] + twice

            rows_loop(0, rows // 2, 4, body)
            level.sweep(PAD, PAD + rows, level.c, level.b)
            level.sweep(PAD, PAD + rows, level.b, level.c)

        down(L2, ny2, L3)
        down(L3, ny3, L4)
        L4.start(PAD, PAD + ny4, L4.b)
        L4.sweep(PAD, PAD + ny4, L4.b, L4.c)

        def twice_4(i, carry):
            L4.sweep(PAD, PAD + ny4, L4.c, L4.b)
            L4.sweep(PAD, PAD + ny4, L4.b, L4.c)
            return carry

        lax.fori_loop(0, (COARSE_SWEEPS - 2) // 2, twice_4, 0)
        up(L3, ny3, L4.c)
        up(L2, ny2, L3.c)

        first2 = PAD + me * (R // 4)
        for j in range(own1 - 3, end1 + 3):
            c1[j] = c1[j] + c2[first2 + (j - H1) // 2]
        L1.sweep(own1 - 2, end1 + 2, c1, b1)
        L1.sweep(own1 - 1, end1 + 1, b1, c1)

        def add_fine(j, c):
            at = pl.ds(2 * j, 2 * c)
            e = c1[pl.ds(j, c)]
            twice = jnp.stack([e, e], axis=1).reshape((2 * c, 8, 128))
            for k in range(2):
                c0[at, k] = c0[at, k] + twice

        rows_loop(own1 - 1, end1 + 1, 5, add_fine)
        sweep0(top - 1, bottom + 1, c0, g0, b0)
        sweep0(top, bottom, b0, g0, dst)

    halo_arrive(start_w, 1)
    vcycle(start_w, gather_1, 1, first_w)
    halo_start(first_w, 2)

    def store_f(s, y):
        f_ref[0, :, s * 256 : (s + 1) * 256] = y

    natural(first_w, top, store_f)
    halo_arrive(first_w, 2)
    vcycle(first_w, gather_2, 2, c0)

    def store_end(s, y):
        end_nat[:, s * 256 : (s + 1) * 256] = y

    natural(c0, top, store_end)
    to_next = pltpu.make_async_remote_copy(
        src_ref=end_nat,
        dst_ref=out_ref.at[0],
        send_sem=end_send,
        recv_sem=end_recv,
        device_id={"tm": lax.rem(mine_t + 1, intervals)},
        device_id_type=MESH,
    )

    @pl.when(mine_t < intervals - 1)
    def _():
        to_next.start()

    @pl.when(mine_t == 0)
    def _():
        out_ref[...] = c_ref[...]

    halo_sent(cond0, 0)
    halo_sent(start_w, 1)
    halo_sent(first_w, 2)
    gather_sent(gather_cond, 0)
    gather_sent(gather_1, 1)
    gather_sent(gather_2, 2)

    @pl.when(mine_t > 0)
    def _():
        to_next.wait_recv()

    @pl.when(mine_t < intervals - 1)
    def _():
        to_next.wait_send()


def pack4(x):
    a, b = pair_rows(x)
    return jnp.where((iota(a.shape, 2) & 1) == 0, a, b)


def unpack4(ref, dst):
    x = ref[...]
    x = x.reshape((x.shape[0] * x.shape[1],) + x.shape[2:])
    even = (iota(x.shape, 2) & 1) == 0
    a = jnp.where(even, x, roll(x, 1, 2))
    b = jnp.where(even, roll(x, 127, 2), x)
    rows = x.shape[0]
    dst[pl.ds(PAD, 2 * rows)] = jnp.stack([a, b], axis=1).reshape((2 * rows,) + x.shape[1:])


def solution(mesh):
    n, intervals = mesh.shape["space"], mesh.shape["tm"]

    def per_device(ids, table, c_points):
        _, R, nx = c_points.shape
        ny = R * n
        window = R + 2 * HALO
        f32 = jnp.float32

        def tiles(*lead):
            return pltpu.VMEM(lead + (8, 128), f32)

        scratch = [pltpu.VMEM((16 * R, 128), f32)]
        names = ["start_w", "first_w", "b0", "c0", "cond0", "fv0", "w0", "e0", "diag0", "om0"]
        for name in names:
            scratch.append(tiles(window) if name == "e0" else tiles(window, 2))
        scratch += [tiles(window // 2) for _ in range(9)]
        for level in (2, 3, 4):
            scratch += [tiles(ny // 2**level + 2 * PAD) for _ in range(9)]
        scratch += [tiles(n, R // 8) for _ in range(3)]
        scratch += [pltpu.VMEM((R, nx), f32)]
        scratch += [
            pltpu.SemaphoreType.DMA((6,)),
            pltpu.SemaphoreType.DMA((6,)),
            pltpu.SemaphoreType.DMA((3 * n,)),
            pltpu.SemaphoreType.DMA((3 * n,)),
            pltpu.SemaphoreType.DMA,
            pltpu.SemaphoreType.DMA,
        ]
        vmem = pl.BlockSpec(memory_space=pltpu.VMEM)
        return pl.pallas_call(
            functools.partial(kernel, n, intervals, ny),
            out_shape=[jax.ShapeDtypeStruct(c_points.shape, f32)] * 2,
            in_specs=[vmem, pl.BlockSpec(memory_space=pltpu.SMEM), vmem],
            out_specs=[vmem, vmem],
            scratch_shapes=scratch,
            compiler_params=pltpu.CompilerParams(
                collective_id=0, has_side_effects=True, vmem_limit_bytes=40 * 1024 * 1024
            ),
        )(ids, table, c_points)

    return jax.shard_map(
        per_device,
        mesh=mesh,
        in_specs=(P("space", None), P(), P("tm", "space", None)),
        out_specs=(P("tm", "space", None), P("tm", "space", None)),
        check_vma=False,
    )
```

profile of v0, /device:TPU:4, one launch (start us, length us, event | category | flops | bytes accessed | tf_op | source)
XLA Modules:
  0.0 45.8 jit_solution(13565629920375081456)
XLA Ops:
  0.6 0.0 copy-start
  0.6 0.9 %copy-done = s32[16,2048]{1,0:T(8,128)S(1)} copy-done((s32[16,2048]{1,0:T(8,128)S(1)}, s32[16,2048]{1,0:T(8,128)}, u32[]{:S(2)}) %copy-start) | copy-done | bytes 131096
  1.5 0.0 copy-start.1
  1.5 0.9 %copy-done.1 = f32[1,16,2048]{2,1,0:T(8,128)S(1)} copy-done((f32[1,16,2048]{2,1,0:T(8,128)S(1)}, f32[1,16,2048]{2,1,0:T(8,128)}, u32[]{:S(2)}) %copy-start.1) | copy-done | bytes 131096
  2.4 0.0 copy-start.2
  2.4 0.7 %copy-done.2 = f32[8]{0:T(128)S(1)} copy-done((f32[8]{0:T(128)S(1)}, f32[8]{0:T(128)}, u32[]{:S(2)}) %copy-start.2) | copy-done | bytes 56
  3.1 41.4 %shard_map.50 = (f32[1,16,2048]{2,1,0:T(8,128)S(1)}, f32[1,16,2048]{2,1,0:T(8,128)S(1)}) custom-call(s32[16,2048]{1,0:T(8,128)S(1)} %copy-done, f32[8]{0:T(128)S(1)} %copy-done.2, f32[1,16,2048]{2,1,0:T(8,128)S(1)} %copy-done.1), custom_call_target="tpu_custom_call" | custom-call | tf_op jit(solution)/shard_map/pallas_call | solution.py:545
  44.5 0.7 %copy.7 = f32[1,16,2048]{2,1,0:T(8,128)} copy(f32[1,16,2048]{2,1,0:T(8,128)S(1)} %get-tuple-element.4) | data formatting | bytes 262144
  45.1 0.7 %copy.8 = f32[1,16,2048]{2,1,0:T(8,128)} copy(f32[1,16,2048]{2,1,0:T(8,128)S(1)} %get-tuple-element.5) | data formatting | bytes 262144
Async XLA Ops:
  0.6 0.9 %copy-start = (s32[16,2048]{1,0:T(8,128)S(1)}, s32[16,2048]{1,0:T(8,128)}, u32[]{:S(2)}) copy-start(s32[16,2048]{1,0:T(8,128)} %ids_ref.1) | copy-start | bytes 393220
  1.5 0.9 %copy-start.1 = (f32[1,16,2048]{2,1,0:T(8,128)S(1)}, f32[1,16,2048]{2,1,0:T(8,128)}, u32[]{:S(2)}) copy-start(f32[1,16,2048]{2,1,0:T(8,128)} %c_ref.1) | copy-start | bytes 393220
  2.4 0.7 %copy-start.2 = (f32[8]{0:T(128)S(1)}, f32[8]{0:T(128)}, u32[]{:S(2)}) copy-start(f32[8]{0:T(128)} %table_ref.1) | copy-start | bytes 100
where the time goes:
time: 46 us; the launch traced here: 45.8 us
  Pallas kernels  41.4 us (90%)
  local copies, waits for them, and re-layouts  3.77 us (8%)
  between operations  0.65 us (1%)
    pallas_call x1, Pallas kernels, per_device(): pl.pallas_call(functools.partial(kernel, n, intervals, ny), out_shape=[ja...  41.4 us
    unnamed x8, local copies, waits for them, and re-layouts  3.77 us

commit v1 on v0

--- a/solution.py
+++ b/solution.py
@@ -143,15 +143,20 @@
 
 def kernel(
     n, intervals, ny,
-    ids_ref, table_ref, c_ref, f_ref, out_ref,
+    ids_hbm, table_ref, c_hbm, f_ref, out_ref,
+    ids_ref, c_ref,
     turn, start_w, first_w, b0, c0, cond0, fv0, w0, e0, diag0, om0,
     cond1, fv1, w1, e1, diag1, om1, g1, b1, c1,
     cond2, fv2, w2, e2, diag2, om2, g2, b2, c2,
     cond3, fv3, w3, e3, diag3, om3, g3, b3, c3,
     cond4, fv4, w4, e4, diag4, om4, g4, b4, c4,
     gather_cond, gather_1, gather_2, end_nat,
-    halo_send, halo_recv, gat_send, gat_recv, end_send, end_recv,
+    halo_send, halo_recv, gat_send, gat_recv, end_send, end_recv, in_sem,
 ):
+    load_ids = pltpu.make_async_copy(ids_hbm, ids_ref, in_sem.at[0])
+    load_c = pltpu.make_async_copy(c_hbm, c_ref, in_sem.at[1])
+    load_ids.start()
+    load_c.start()
     me = lax.axis_index("space")
     mine_t = lax.axis_index("tm")
     R = c_ref.shape[1]
@@ -259,6 +264,7 @@
     def chunks(x):
         return jnp.concatenate([x[:, s * 256 : (s + 1) * 256] for s in range(8)], axis=0)
 
+    load_ids.wait()
     put_turned(dot(chunks(ids_ref[...].astype(jnp.float32)).astype(jnp.bfloat16), into))
     for r in range(R):
         for k in range(2):
@@ -268,32 +274,32 @@
                 value = jnp.where(kind == float(m), table_ref[m], value)
             cond0[top + r, k] = value
 
+    def natural(src, row0, rows, base, store):
+        for r in range(rows):
+            for k in range(2):
+                turn[pl.ds(base + k * 8 * rows + r, 8, stride=rows), :] = src[row0 + r, k]
+        back = jnp.where(row_i == (col_i & 1) * 128 + (col_i >> 1), 1.0, 0.0).astype(jnp.bfloat16)
+        x = jnp.concatenate(
+            [turn[pl.ds(base, 8 * rows), :], turn[pl.ds(base + 8 * rows, 8 * rows), :]], axis=1
+        )
+        y = sum(dot(part, back) for part in split3(x))
+        for s in range(8):
+            store(s, y[s * rows : (s + 1) * rows])
+
+    pl.semaphore_wait(barrier, n + 1)
+
+    halo_start(cond0, 0)
+    load_c.wait()
     put_turned(sum(dot(part, into) for part in split3(chunks(c_ref[0]))))
     for r in range(R):
         for k in range(2):
             start_w[top + r, k] = turn[pl.ds(k * 8 * R + r, 8, stride=R), :]
-
-    def natural(src, row0, store):
-        for r in range(R):
-            for k in range(2):
-                turn[pl.ds(k * 8 * R + r, 8, stride=R), :] = src[row0 + r, k]
-        back = jnp.where(row_i == (col_i & 1) * 128 + (col_i >> 1), 1.0, 0.0).astype(jnp.bfloat16)
-        x = jnp.concatenate(
-            [turn[pl.ds(0, 8 * R), :], turn[pl.ds(8 * R, 8 * R), :]], axis=1
-        )
-        y = sum(dot(part, back) for part in split3(x))
-        for s in range(8):
-            store(s, y[s * R : (s + 1) * R])
-
-    pl.semaphore_wait(barrier, n + 1)
-
-    halo_start(cond0, 0)
     halo_start(start_w, 1)
 
     scale = DIFFUSION
     L1 = Level((cond1, fv1, w1, e1, diag1, om1, g1, b1, c1), 1, scale / 4, 7)
-    L2 = Level((cond2, fv2, w2, e2, diag2, om2, g2, b2, c2), 2, scale / 16, 8)
-    L3 = Level((cond3, fv3, w3, e3, diag3, om3, g3, b3, c3), 4, scale / 64, 8)
+    L2 = Level((cond2, fv2, w2, e2, diag2, om2, g2, b2, c2), 2, scale / 16, 16)
+    L3 = Level((cond3, fv3, w3, e3, diag3, om3, g3, b3, c3), 4, scale / 64, 16)
     L4 = Level((cond4, fv4, w4, e4, diag4, om4, g4, b4, c4), 8, scale / 256, 8)
     ny2, ny3, ny4 = ny // 4, ny // 8, ny // 16
 
@@ -315,13 +321,6 @@
         for ref in (level.cond, level.b, level.c, level.fv):
             ref[pl.ds(0, PAD)] = zero_pad
             ref[pl.ds(PAD + rows, PAD)] = zero_pad
-
-    gather_arrive(gather_cond, 0)
-    unpack4(gather_cond, cond2)
-    cond3[pl.ds(PAD, ny3)] = restrict(cond2[pl.ds(PAD, ny2)], 2)
-    cond4[pl.ds(PAD, ny4)] = restrict(cond3[pl.ds(PAD, ny3)], 4)
-    for level, rows in ((L2, ny2), (L3, ny3), (L4, ny4)):
-        level.setup(PAD, PAD + rows, 0, rows - 1, -PAD)
 
     halo_arrive(cond0, 0)
     coarsen_cond(0, H1)
@@ -352,6 +351,14 @@
     rows_loop(1, window - 1, 4, setup0)
     L1.setup(1, R // 2 + 2 * H1 - 1, 0, ny // 2 - 1, me * (R // 2) - H1)
 
+    def setup_low():
+        gather_arrive(gather_cond, 0)
+        unpack4(gather_cond, cond2)
+        cond3[pl.ds(PAD, ny3)] = restrict(cond2[pl.ds(PAD, ny2)], 2)
+        cond4[pl.ds(PAD, ny4)] = restrict(cond3[pl.ds(PAD, ny3)], 4)
+        for level, rows in ((L2, ny2), (L3, ny3), (L4, ny4)):
+            level.setup(PAD, PAD + rows, 0, rows - 1, -PAD)
+
     def beside0(v, r, c):
         v0, v1 = v[pl.ds(r, c), 0], v[pl.ds(r, c), 1]
         up, down = pl.ds(r - 1, c), pl.ds(r + 1, c)
@@ -372,11 +379,16 @@
             for k in range(2):
                 dst[at, k] = 0.2 * here[k] + om0[at, k] * (g[at, k] + nb[k])
 
-        rows_loop(lo, hi, 6, body)
+        rows_loop(lo, hi, {14: 7, 8: 8, 16: 8}.get(hi - lo, 6), body)
 
     def vcycle(g0, gathered, which, dst):
-        sweep0(top - 10, bottom + 10, g0, g0, b0)
-        sweep0(top - 9, bottom + 9, b0, g0, c0)
+        sweep0(top + 1, bottom - 1, g0, g0, b0)
+        sweep0(top + 2, bottom - 2, b0, g0, c0)
+        halo_arrive(g0, which)
+        sweep0(top - 10, top + 1, g0, g0, b0)
+        sweep0(bottom - 1, bottom + 10, g0, g0, b0)
+        sweep0(top - 9, top + 2, b0, g0, c0)
+        sweep0(bottom - 2, bottom + 9, b0, g0, c0)
 
         def to_level_1(j, c):
             r, rows = 2 * j, 2 * c
@@ -393,6 +405,8 @@
         L1.sweep(own1 - 3, end1 + 3, b1, c1)
         gathered[me] = pack4(restrict(L1.residue(c1, own1, R // 2), 1))
         gather_start(gathered, which)
+        if which == 1:
+            setup_low()
         gather_arrive(gathered, which)
         unpack4(gathered, g2)
 
@@ -405,7 +419,7 @@
                     level.residue(level.c, PAD + 2 * j, 2 * c), level.d
                 )
 
-            rows_loop(0, rows // 2, 4, body)
+            rows_loop(0, rows // 2, 8, body)
 
         def up(level, rows, e_ref):
             def body(j, c):
@@ -414,7 +428,7 @@
                 twice = jnp.stack([e, e], axis=1).reshape((2 * c, 8, 128))
                 level.c[at] = level.c[at] + twice
 
-            rows_loop(0, rows // 2, 4, body)
+            rows_loop(0, rows // 2, 8, body)
             level.sweep(PAD, PAD + rows, level.c, level.b)
             level.sweep(PAD, PAD + rows, level.b, level.c)
 
@@ -447,35 +461,41 @@
 
         rows_loop(own1 - 1, end1 + 1, 5, add_fine)
         sweep0(top - 1, bottom + 1, c0, g0, b0)
-        sweep0(top, bottom, b0, g0, dst)
-
-    halo_arrive(start_w, 1)
+        if which == 1:
+            sweep0(top, bottom, b0, g0, dst)
+
     vcycle(start_w, gather_1, 1, first_w)
     halo_start(first_w, 2)
 
     def store_f(s, y):
         f_ref[0, :, s * 256 : (s + 1) * 256] = y
 
-    natural(first_w, top, store_f)
-    halo_arrive(first_w, 2)
+    natural(first_w, top, R, 0, store_f)
     vcycle(first_w, gather_2, 2, c0)
 
-    def store_end(s, y):
-        end_nat[:, s * 256 : (s + 1) * 256] = y
-
-    natural(c0, top, store_end)
-    to_next = pltpu.make_async_remote_copy(
-        src_ref=end_nat,
-        dst_ref=out_ref.at[0],
-        send_sem=end_send,
-        recv_sem=end_recv,
-        device_id={"tm": lax.rem(mine_t + 1, intervals)},
-        device_id_type=MESH,
-    )
-
-    @pl.when(mine_t < intervals - 1)
-    def _():
-        to_next.start()
+    half = R // 2
+
+    def to_next(h):
+        return pltpu.make_async_remote_copy(
+            src_ref=end_nat.at[pl.ds(h * half, half)],
+            dst_ref=out_ref.at[0, pl.ds(h * half, half)],
+            send_sem=end_send.at[h],
+            recv_sem=end_recv.at[h],
+            device_id={"tm": lax.rem(mine_t + 1, intervals)},
+            device_id_type=MESH,
+        )
+
+    for h in range(2):
+        sweep0(top + h * half, top + (h + 1) * half, b0, first_w, c0)
+
+        def store_end(s, y, h=h):
+            end_nat[h * half : (h + 1) * half, s * 256 : (s + 1) * 256] = y
+
+        natural(c0, top + h * half, half, h * 8 * R, store_end)
+
+        @pl.when(mine_t < intervals - 1)
+        def _(h=h):
+            to_next(h).start()
 
     @pl.when(mine_t == 0)
     def _():
@@ -490,11 +510,13 @@
 
     @pl.when(mine_t > 0)
     def _():
-        to_next.wait_recv()
+        for h in range(2):
+            to_next(h).wait_recv()
 
     @pl.when(mine_t < intervals - 1)
     def _():
-        to_next.wait_send()
+        for h in range(2):
+            to_next(h).wait_send()
 
 
 def pack4(x):
@@ -524,7 +546,8 @@
         def tiles(*lead):
             return pltpu.VMEM(lead + (8, 128), f32)
 
-        scratch = [pltpu.VMEM((16 * R, 128), f32)]
+        scratch = [pltpu.VMEM(ids.shape, ids.dtype), pltpu.VMEM(c_points.shape, f32)]
+        scratch += [pltpu.VMEM((16 * R, 128), f32)]
         names = ["start_w", "first_w", "b0", "c0", "cond0", "fv0", "w0", "e0", "diag0", "om0"]
         for name in names:
             scratch.append(tiles(window) if name == "e0" else tiles(window, 2))
@@ -538,14 +561,16 @@
             pltpu.SemaphoreType.DMA((6,)),
             pltpu.SemaphoreType.DMA((3 * n,)),
             pltpu.SemaphoreType.DMA((3 * n,)),
-            pltpu.SemaphoreType.DMA,
-            pltpu.SemaphoreType.DMA,
+            pltpu.SemaphoreType.DMA((2,)),
+            pltpu.SemaphoreType.DMA((2,)),
+            pltpu.SemaphoreType.DMA((2,)),
         ]
+        hbm = pl.BlockSpec(memory_space=pltpu.HBM)
         vmem = pl.BlockSpec(memory_space=pltpu.VMEM)
         return pl.pallas_call(
             functools.partial(kernel, n, intervals, ny),
             out_shape=[jax.ShapeDtypeStruct(c_points.shape, f32)] * 2,
-            in_specs=[vmem, pl.BlockSpec(memory_space=pltpu.SMEM), vmem],
+            in_specs=[hbm, pl.BlockSpec(memory_space=pltpu.SMEM), hbm],
             out_specs=[vmem, vmem],
             scratch_shapes=scratch,
             compiler_params=pltpu.CompilerParams(

time: 46 us -> 38.8 us (0.84)
  Pallas kernels: 41.4 us -> 34.2 us
    pallas_call x1, Pallas kernels: 41.4 us -> 34.2 us  [per_device(): pl.pallas_call(functools.partial(kernel, n, intervals, ny), out_shape=[ja...]
where the time goes in v1:
time: 38.8 us; the launch traced here: 38.7 us
  Pallas kernels  34.2 us (88%)
  local copies, waits for them, and re-layouts  3.77 us (10%)
  between operations  0.65 us (2%)
    pallas_call x1, Pallas kernels, per_device(): pl.pallas_call(functools.partial(kernel, n, intervals, ny), out_shape=[ja...  34.2 us
    unnamed x8, local copies, waits for them, and re-layouts  3.77 us

profile of v1, /device:TPU:4, one launch (start us, length us, event | category | flops | bytes accessed | tf_op | source)
XLA Modules:
  0.0 38.7 jit_solution(17591882707605600049)
XLA Ops:
  0.6 0.0 copy-start
  0.6 0.9 %copy-done = s32[16,2048]{1,0:T(8,128)S(1)} copy-done((s32[16,2048]{1,0:T(8,128)S(1)}, s32[16,2048]{1,0:T(8,128)}, u32[]{:S(2)}) %copy-start) | copy-done | bytes 131096
  1.5 0.0 copy-start.1
  1.5 0.9 %copy-done.1 = f32[1,16,2048]{2,1,0:T(8,128)S(1)} copy-done((f32[1,16,2048]{2,1,0:T(8,128)S(1)}, f32[1,16,2048]{2,1,0:T(8,128)}, u32[]{:S(2)}) %copy-start.1) | copy-done | bytes 131096
  2.4 0.0 copy-start.2
  2.4 0.7 %copy-done.2 = f32[8]{0:T(128)S(1)} copy-done((f32[8]{0:T(128)S(1)}, f32[8]{0:T(128)}, u32[]{:S(2)}) %copy-start.2) | copy-done | bytes 56
  3.1 34.2 %shard_map.50 = (f32[1,16,2048]{2,1,0:T(8,128)S(1)}, f32[1,16,2048]{2,1,0:T(8,128)S(1)}) custom-call(s32[16,2048]{1,0:T(8,128)S(1)} %copy-done, f32[8]{0:T(128)S(1)} %copy-done.2, f32[1,16,2048]{2,1,0:T(8,128)S(1)} %copy-done.1), custom_call_target="tpu_custom_call" | custom-call | tf_op jit(solution)/shard_map/pallas_call | solution.py:570
  37.4 0.7 %copy.7 = f32[1,16,2048]{2,1,0:T(8,128)} copy(f32[1,16,2048]{2,1,0:T(8,128)S(1)} %get-tuple-element.4) | data formatting | bytes 262144
  38.0 0.7 %copy.8 = f32[1,16,2048]{2,1,0:T(8,128)} copy(f32[1,16,2048]{2,1,0:T(8,128)S(1)} %get-tuple-element.5) | data formatting | bytes 262144
Async XLA Ops:
  0.6 0.9 %copy-start = (s32[16,2048]{1,0:T(8,128)S(1)}, s32[16,2048]{1,0:T(8,128)}, u32[]{:S(2)}) copy-start(s32[16,2048]{1,0:T(8,128)} %ids_hbm.1) | copy-start | bytes 393220
  1.5 0.9 %copy-start.1 = (f32[1,16,2048]{2,1,0:T(8,128)S(1)}, f32[1,16,2048]{2,1,0:T(8,128)}, u32[]{:S(2)}) copy-start(f32[1,16,2048]{2,1,0:T(8,128)} %c_hbm.1) | copy-start | bytes 393220
  2.4 0.7 %copy-start.2 = (f32[8]{0:T(128)S(1)}, f32[8]{0:T(128)}, u32[]{:S(2)}) copy-start(f32[8]{0:T(128)} %table_ref.1) | copy-start | bytes 100

commit v2 on v1

--- a/solution.py
+++ b/solution.py
@@ -83,6 +83,49 @@
 
 def dot(a, b):
     return jnp.dot(a, b, preferred_element_type=jnp.float32)
+
+
+def compact(x):
+    keep = (iota(x.shape, 2) & 7) == iota(x.shape, 1)
+    return jnp.sum(jnp.where(keep, x, 0.0), axis=1)
+
+
+def spread(x):
+    shape = (x.shape[0], 8, 128)
+    y = jnp.broadcast_to(x[:, None, :], shape)
+    y = jnp.where((iota(shape, 2) & 7) == iota(shape, 1), y, 0.0)
+    for d in (1, 2, 4):
+        y = y + partner(y, d)
+    return y
+
+
+def coarsest(cond, scale):
+    half, shape, rows = 0.5 * scale, cond.shape, cond.shape[0]
+    row, lane = iota(shape, 0), iota(shape, 1)
+
+    def west_of(v):
+        return jnp.where(lane < 8, roll(v, 9, 1), roll(v, 8, 1))
+
+    def east_of(v):
+        return jnp.where(lane >= 120, roll(v, 119, 1), roll(v, 120, 1))
+
+    def north_of(v):
+        return roll(v, 1, 0)
+
+    def south_of(v):
+        return roll(v, rows - 1, 0)
+
+    moves = (north_of, south_of, west_of, east_of)
+    outside = (row == 0, row == rows - 1, lane == 0, lane == 127)
+    faces, masked = [], []
+    for move, out in zip(moves, outside):
+        face = half * (cond + jnp.where(out, 0.0, move(cond)))
+        faces.append(face)
+        masked.append(jnp.where(out, 0.0, face))
+    north, south, west, east = faces
+    diag = 1.0 + ((north + south) + (west + east))
+    om = 0.8 / diag
+    return moves, [om * m for m in masked], om
 
 
 class Level:
@@ -149,7 +192,7 @@
     cond1, fv1, w1, e1, diag1, om1, g1, b1, c1,
     cond2, fv2, w2, e2, diag2, om2, g2, b2, c2,
     cond3, fv3, w3, e3, diag3, om3, g3, b3, c3,
-    cond4, fv4, w4, e4, diag4, om4, g4, b4, c4,
+    g4, c4, om4, n4, s4, w4, e4,
     gather_cond, gather_1, gather_2, end_nat,
     halo_send, halo_recv, gat_send, gat_recv, end_send, end_recv, in_sem,
 ):
@@ -297,10 +340,9 @@
     halo_start(start_w, 1)
 
     scale = DIFFUSION
-    L1 = Level((cond1, fv1, w1, e1, diag1, om1, g1, b1, c1), 1, scale / 4, 7)
-    L2 = Level((cond2, fv2, w2, e2, diag2, om2, g2, b2, c2), 2, scale / 16, 16)
+    L1 = Level((cond1, fv1, w1, e1, diag1, om1, g1, b1, c1), 1, scale / 4, 16)
+    L2 = Level((cond2, fv2, w2, e2, diag2, om2, g2, b2, c2), 2, scale / 16, 32)
     L3 = Level((cond3, fv3, w3, e3, diag3, om3, g3, b3, c3), 4, scale / 64, 16)
-    L4 = Level((cond4, fv4, w4, e4, diag4, om4, g4, b4, c4), 8, scale / 256, 8)
     ny2, ny3, ny4 = ny // 4, ny // 8, ny // 16
 
     def coarsen_cond(lo, hi):
@@ -317,7 +359,7 @@
     gather_start(gather_cond, 0)
 
     zero_pad = jnp.zeros((PAD, 8, 128), jnp.float32)
-    for level, rows in ((L2, ny2), (L3, ny3), (L4, ny4)):
+    for level, rows in ((L2, ny2), (L3, ny3)):
         for ref in (level.cond, level.b, level.c, level.fv):
             ref[pl.ds(0, PAD)] = zero_pad
             ref[pl.ds(PAD + rows, PAD)] = zero_pad
@@ -348,15 +390,18 @@
         w0[pl.ds(r, c), 1] = mid
         e0[pl.ds(r, c)] = jnp.where(out_e, 0.0, east)
 
-    rows_loop(1, window - 1, 4, setup0)
+    rows_loop(1, window - 1, 10, setup0)
     L1.setup(1, R // 2 + 2 * H1 - 1, 0, ny // 2 - 1, me * (R // 2) - H1)
 
     def setup_low():
         gather_arrive(gather_cond, 0)
         unpack4(gather_cond, cond2)
         cond3[pl.ds(PAD, ny3)] = restrict(cond2[pl.ds(PAD, ny2)], 2)
-        cond4[pl.ds(PAD, ny4)] = restrict(cond3[pl.ds(PAD, ny3)], 4)
-        for level, rows in ((L2, ny2), (L3, ny3), (L4, ny4)):
+        _, sides, om = coarsest(compact(restrict(cond3[pl.ds(PAD, ny3)], 4)), scale / 256)
+        om4[...] = om
+        for ref, side in zip((n4, s4, w4, e4), sides):
+            ref[...] = side
+        for level, rows in ((L2, ny2), (L3, ny3)):
             level.setup(PAD, PAD + rows, 0, rows - 1, -PAD)
 
     def beside0(v, r, c):
@@ -379,7 +424,7 @@
             for k in range(2):
                 dst[at, k] = 0.2 * here[k] + om0[at, k] * (g[at, k] + nb[k])
 
-        rows_loop(lo, hi, {14: 7, 8: 8, 16: 8}.get(hi - lo, 6), body)
+        rows_loop(lo, hi, {14: 14, 8: 8, 16: 16, 18: 9}.get(hi - lo, 12), body)
 
     def vcycle(g0, gathered, which, dst):
         sweep0(top + 1, bottom - 1, g0, g0, b0)
@@ -400,7 +445,7 @@
             g1[pl.ds(j, c)] = 0.25 * (a + b)
 
         own1, end1 = H1, H1 + R // 2
-        rows_loop(own1 - 4, end1 + 4, 4, to_level_1)
+        rows_loop(own1 - 4, end1 + 4, 8, to_level_1)
         L1.start(own1 - 4, end1 + 4, b1)
         L1.sweep(own1 - 3, end1 + 3, b1, c1)
         gathered[me] = pack4(restrict(L1.residue(c1, own1, R // 2), 1))
@@ -410,16 +455,16 @@
         gather_arrive(gathered, which)
         unpack4(gathered, g2)
 
-        def down(level, rows, coarse):
+        def down(level, rows, coarse_g):
             level.start(PAD, PAD + rows, level.b)
             level.sweep(PAD, PAD + rows, level.b, level.c)
 
             def body(j, c):
-                coarse.g[pl.ds(PAD + j, c)] = restrict(
+                coarse_g[pl.ds(PAD + j, c)] = restrict(
                     level.residue(level.c, PAD + 2 * j, 2 * c), level.d
                 )
 
-            rows_loop(0, rows // 2, 8, body)
+            rows_loop(0, rows // 2, 16, body)
 
         def up(level, rows, e_ref):
             def body(j, c):
@@ -428,22 +473,25 @@
                 twice = jnp.stack([e, e], axis=1).reshape((2 * c, 8, 128))
                 level.c[at] = level.c[at] + twice
 
-            rows_loop(0, rows // 2, 8, body)
+            rows_loop(0, rows // 2, 16, body)
             level.sweep(PAD, PAD + rows, level.c, level.b)
             level.sweep(PAD, PAD + rows, level.b, level.c)
 
-        down(L2, ny2, L3)
-        down(L3, ny3, L4)
-        L4.start(PAD, PAD + ny4, L4.b)
-        L4.sweep(PAD, PAD + ny4, L4.b, L4.c)
-
-        def twice_4(i, carry):
-            L4.sweep(PAD, PAD + ny4, L4.c, L4.b)
-            L4.sweep(PAD, PAD + ny4, L4.b, L4.c)
-            return carry
-
-        lax.fori_loop(0, (COARSE_SWEEPS - 2) // 2, twice_4, 0)
-        up(L3, ny3, L4.c)
+        down(L2, ny2, g3)
+        down(L3, ny3, g4)
+        lane = iota((ny4, 128), 1)
+        first = om4[...] * compact(g4[pl.ds(PAD, ny4)])
+
+        def sweep4(i, v):
+            west = jnp.where(lane < 8, roll(v, 9, 1), roll(v, 8, 1))
+            east = jnp.where(lane >= 120, roll(v, 119, 1), roll(v, 120, 1))
+            nb = (n4[...] * roll(v, 1, 0) + s4[...] * roll(v, ny4 - 1, 0)) + (
+                w4[...] * west + e4[...] * east
+            )
+            return (0.2 * v + first) + nb
+
+        c4[pl.ds(PAD, ny4)] = spread(lax.fori_loop(0, COARSE_SWEEPS - 1, sweep4, first, unroll=5))
+        up(L3, ny3, c4)
         up(L2, ny2, L3.c)
 
         first2 = PAD + me * (R // 4)
@@ -459,7 +507,7 @@
             for k in range(2):
                 c0[at, k] = c0[at, k] + twice
 
-        rows_loop(own1 - 1, end1 + 1, 5, add_fine)
+        rows_loop(own1 - 1, end1 + 1, 10, add_fine)
         sweep0(top - 1, bottom + 1, c0, g0, b0)
         if which == 1:
             sweep0(top, bottom, b0, g0, dst)
@@ -552,8 +600,10 @@
         for name in names:
             scratch.append(tiles(window) if name == "e0" else tiles(window, 2))
         scratch += [tiles(window // 2) for _ in range(9)]
-        for level in (2, 3, 4):
+        for level in (2, 3):
             scratch += [tiles(ny // 2**level + 2 * PAD) for _ in range(9)]
+        scratch += [tiles(ny // 16 + 2 * PAD) for _ in range(2)]
+        scratch += [pltpu.VMEM((ny // 16, 128), f32) for _ in range(5)]
         scratch += [tiles(n, R // 8) for _ in range(3)]
         scratch += [pltpu.VMEM((R, nx), f32)]
         scratch += [

time: 38.8 us -> 36.6 us (0.943)
  Pallas kernels: 34.2 us -> 32 us
    pallas_call x1, Pallas kernels: 34.2 us -> 32 us  [per_device(): pl.pallas_call(functools.partial(kernel, n, intervals, ny), out_shape=[ja...]
where the time goes in v2:
time: 36.6 us; the launch traced here: 36.4 us
  Pallas kernels  32 us (87%)
  local copies, waits for them, and re-layouts  3.77 us (10%)
  between operations  0.65 us (2%)
    pallas_call x1, Pallas kernels, per_device(): pl.pallas_call(functools.partial(kernel, n, intervals, ny), out_shape=[ja...  32 us
    unnamed x8, local copies, waits for them, and re-layouts  3.77 us

profile of v2, /device:TPU:4, one launch (start us, length us, event | category | flops | bytes accessed | tf_op | source)
XLA Modules:
  0.0 36.4 jit_solution(12853111503546784534)
XLA Ops:
  0.6 0.0 copy-start
  0.6 0.9 %copy-done = s32[16,2048]{1,0:T(8,128)S(1)} copy-done((s32[16,2048]{1,0:T(8,128)S(1)}, s32[16,2048]{1,0:T(8,128)}, u32[]{:S(2)}) %copy-start) | copy-done | bytes 131096
  1.5 0.0 copy-start.1
  1.5 0.9 %copy-done.1 = f32[1,16,2048]{2,1,0:T(8,128)S(1)} copy-done((f32[1,16,2048]{2,1,0:T(8,128)S(1)}, f32[1,16,2048]{2,1,0:T(8,128)}, u32[]{:S(2)}) %copy-start.1) | copy-done | bytes 131096
  2.4 0.0 copy-start.2
  2.4 0.7 %copy-done.2 = f32[8]{0:T(128)S(1)} copy-done((f32[8]{0:T(128)S(1)}, f32[8]{0:T(128)}, u32[]{:S(2)}) %copy-start.2) | copy-done | bytes 56
  3.1 32.0 %shard_map.50 = (f32[1,16,2048]{2,1,0:T(8,128)S(1)}, f32[1,16,2048]{2,1,0:T(8,128)S(1)}) custom-call(s32[16,2048]{1,0:T(8,128)S(1)} %copy-done, f32[8]{0:T(128)S(1)} %copy-done.2, f32[1,16,2048]{2,1,0:T(8,128)S(1)} %copy-done.1), custom_call_target="tpu_custom_call" | custom-call | tf_op jit(solution)/shard_map/pallas_call | solution.py:620
  35.1 0.7 %copy.7 = f32[1,16,2048]{2,1,0:T(8,128)} copy(f32[1,16,2048]{2,1,0:T(8,128)S(1)} %get-tuple-element.4) | data formatting | bytes 262144
  35.8 0.7 %copy.8 = f32[1,16,2048]{2,1,0:T(8,128)} copy(f32[1,16,2048]{2,1,0:T(8,128)S(1)} %get-tuple-element.5) | data formatting | bytes 262144
Async XLA Ops:
  0.6 0.9 %copy-start = (s32[16,2048]{1,0:T(8,128)S(1)}, s32[16,2048]{1,0:T(8,128)}, u32[]{:S(2)}) copy-start(s32[16,2048]{1,0:T(8,128)} %ids_hbm.1) | copy-start | bytes 393220
  1.5 0.9 %copy-start.1 = (f32[1,16,2048]{2,1,0:T(8,128)S(1)}, f32[1,16,2048]{2,1,0:T(8,128)}, u32[]{:S(2)}) copy-start(f32[1,16,2048]{2,1,0:T(8,128)} %c_hbm.1) | copy-start | bytes 393220
  2.4 0.7 %copy-start.2 = (f32[8]{0:T(128)S(1)}, f32[8]{0:T(128)}, u32[]{:S(2)}) copy-start(f32[8]{0:T(128)} %table_ref.1) | copy-start | bytes 100
